TPU v7x, 256 devices: a whole 4x4x8 slice. The times are simulated.
256 devices in a mesh: dp: 4 (over x), expert: 64 (over y, z, core).
Axes of the slice: x: 4, y: 4, z: 8, core: 2. Of those that a mesh axis runs over, the one named last changes fastest.
Arguments:
- saved_input: bfloat16 [8192, 2048], P(('dp', 'expert')), may hold values from -6 to 6
- output_grad: bfloat16 [8192, 2048], P(('dp', 'expert')), may hold values from -6 to 6
- route_probs: float32 [8192, 8], P(('dp', 'expert')), may hold values from 0.02 to 0.4
- expert_choice: int32 [8192, 8], P(('dp', 'expert')), may hold values from 0 to 127, all different within a row; in each aligned block of 32 rows (0 to 31, 32 to 63, ...) at most 3 rows name the same one
- slot_expert: int32 [4, 64], replicated, may hold values from 0 to 127, as said below
- frozen_gate: bfloat16 [256, 2048, 768], P(('dp', 'expert')), as said below
- frozen_up: bfloat16 [256, 2048, 768], P(('dp', 'expert')), as said below
- frozen_down: bfloat16 [256, 768, 2048], P(('dp', 'expert')), as said below
- adapter_in: float32 [128, 64, 768], P('expert', 'dp'), may hold values from -0.21875 to 0.21875
- adapter_out: float32 [128, 64, 2048], P('expert', 'dp'), may hold values from -0.125 to 0.125
- moment_in: float32 [128, 64, 768], P('expert', 'dp'), may hold values from -3 to 3
- moment_out: float32 [128, 64, 2048], P('expert', 'dp'), may hold values from -3 to 3
- second_in: float32 [128, 64, 768], P('expert', 'dp'), may hold values from 0.01 to 1
- second_out: float32 [128, 64, 2048], P('expert', 'dp'), may hold values from 0.01 to 1
Outputs:
- input_grad: bfloat16 [8192, 2048], P(('dp', 'expert'))
- step_in: float32 [128, 64, 768], P('expert', 'dp')
- step_out: float32 [128, 64, 2048], P('expert', 'dp')
- momentum_in: float32 [128, 64, 768], P('expert', 'dp')
- momentum_out: float32 [128, 64, 2048], P('expert', 'dp')
- variance_in: float32 [128, 64, 768], P('expert', 'dp')
- variance_out: float32 [128, 64, 2048], P('expert', 'dp')
- replica_in: bfloat16 [256, 64, 768], P(('dp', 'expert'))
- replica_out: bfloat16 [256, 64, 2048], P(('dp', 'expert'))
Inputs may be any that keep to these rules, and one draw needn't show every extreme that they name: `expert_choice`: among the rows of one device no expert is named more than 3 times. `slot_expert`: the slots of index j of the expert axis host only experts 2 * j to 2 * j + 1, and each of these at least once. `frozen_gate`: slots that host the same expert hold the same frozen weights. `frozen_up`: slots that host the same expert hold the same frozen weights. `frozen_down`: slots that host the same expert hold the same frozen weights.
All inputs are finite; a program needn't handle non-finite values.
Results may differ from a plain program's by a relative error of at most 0.012.
Values may be sent and summed in bfloat16 or wider, within the bound.
A program may use at most 128 MiB of HBM per device.

v0:
```python
import jax
import jax.numpy as jnp
from jax import lax
from jax.sharding import PartitionSpec as P

STEP = 100
adapter_scale_factor = 2.0
beta_one = 0.9
beta_two = 0.999
decay_rate = 0.01
adam_eps = 1e-08


def contract_product(left, right, left_dim, right_dim):
    return lax.dot_general(
        left, right, (((left_dim,), (right_dim,)), ((), ())), preferred_element_type=jnp.float32
    )


def route_rows(choice_flat, slot_expert, source, local_experts):
    column = choice_flat // local_experts
    hosted = (jnp.take(slot_expert, column, axis=1) == choice_flat[None, :]).astype(jnp.int32)
    counts = jnp.sum(hosted, axis=0)
    picked = source % counts
    running = jnp.cumsum(hosted, axis=0) - 1
    chosen = hosted * (running == picked[None, :]).astype(jnp.int32)
    dp_ids = jnp.arange(hosted.shape[0], dtype=jnp.int32)
    dest_row = jnp.sum(chosen * dp_ids[:, None], axis=0)
    row_ids = jnp.arange(choice_flat.shape[0], dtype=jnp.int32)
    earlier = (choice_flat[None, :] == choice_flat[:, None]) & (row_ids[None, :] < row_ids[:, None])
    rank = jnp.sum(earlier.astype(jnp.int32), axis=1)
    return (dest_row, column, rank)


def pack_rows(saved_input, scaled, position, buffer_size, top_count, shape_out):
    row_count = scaled.shape[0]
    row_ids = jnp.arange(row_count, dtype=jnp.int32)
    filler = jnp.full((buffer_size,), row_count, jnp.int32).at[position].set(row_ids)
    send_input = jnp.take(saved_input, filler // top_count, axis=0, mode="fill", fill_value=0)
    send_grad = jnp.take(scaled, filler, axis=0, mode="fill", fill_value=0)
    return (send_input.reshape(shape_out), send_grad.reshape(shape_out))


def adamw(param, grad, first, second):
    first_new = beta_one * first + (1.0 - beta_one) * grad
    second_new = beta_two * second + (1.0 - beta_two) * grad * grad
    corr_one = 1.0 - beta_one**STEP
    corr_two = 1.0 - beta_two**STEP
    step_dir = (
        first_new / corr_one / (jnp.sqrt(second_new / corr_two) + adam_eps) + decay_rate * param
    )
    return (step_dir, first_new, second_new)


def per_device(
    saved_input,
    output_grad,
    route_probs,
    expert_choice,
    slot_expert,
    frozen_gate,
    frozen_up,
    frozen_down,
    adapter_in,
    adapter_out,
    moment_in,
    moment_out,
    second_in,
    second_out,
):
    dp_count = lax.axis_size("dp")
    expert_count = lax.axis_size("expert")
    dp_index = lax.axis_index("dp")
    column_index = lax.axis_index("expert")
    local_experts = adapter_in.shape[0]
    token_count, top_count = expert_choice.shape
    width = saved_input.shape[1]
    row_count = token_count * top_count
    capacity = max(2, -(-3 * row_count // (2 * local_experts * expert_count)))
    buffer_size = dp_count * expert_count * capacity
    source = dp_index * expert_count + column_index
    choice_flat = expert_choice.reshape(row_count)
    dest_row, column, rank = route_rows(choice_flat, slot_expert, source, local_experts)
    scaled = (
        (route_probs[:, :, None] * output_grad[:, None, :].astype(jnp.float32))
        .astype(jnp.bfloat16)
        .reshape(row_count, width)
    )
    slot_shape = (dp_count, expert_count, capacity, width)
    position = (dest_row * expert_count + column) * capacity + rank
    send_input, send_grad = pack_rows(
        saved_input, scaled, position, buffer_size, top_count, slot_shape
    )
    arrived_input, arrived_grad = (
        lax.all_to_all(
            lax.all_to_all(send_input, "dp", split_axis=0, concat_axis=0, tiled=True),
            "expert",
            split_axis=1,
            concat_axis=1,
            tiled=True,
        ),
        lax.all_to_all(
            lax.all_to_all(send_grad, "dp", split_axis=0, concat_axis=0, tiled=True),
            "expert",
            split_axis=1,
            concat_axis=1,
            tiled=True,
        ),
    )
    fetched_in, fetched_out = (
        lax.all_gather(adapter_in.astype(jnp.bfloat16), "dp", axis=1, tiled=True),
        lax.all_gather(adapter_out.astype(jnp.bfloat16), "dp", axis=1, tiled=True),
    )
    hosted_local = slot_expert[dp_index, column_index] - local_experts * column_index
    owned_input = lax.dynamic_index_in_dim(fetched_in, hosted_local, 0, keepdims=False)
    own_out = lax.dynamic_index_in_dim(fetched_out, hosted_local, 0, keepdims=False)
    buffer_rows = arrived_input.reshape(buffer_size, width)
    gradient_row_block = arrived_grad.reshape(buffer_size, width)
    gate_weight = frozen_gate[0]
    up_weight = frozen_up[0]
    down_weight = frozen_down[0]
    gate_pre = jnp.dot(buffer_rows, gate_weight, preferred_element_type=jnp.float32)
    up_pre = jnp.dot(buffer_rows, up_weight, preferred_element_type=jnp.float32)
    sigmoid_gate = jax.nn.sigmoid(gate_pre)
    hidden_state = (gate_pre * sigmoid_gate * up_pre).astype(jnp.bfloat16)
    low_rank_input = contract_product(hidden_state, owned_input, 1, 1).astype(jnp.bfloat16)
    low_rank_gradient = contract_product(gradient_row_block, own_out, 1, 1).astype(jnp.bfloat16)
    hidden_gradient = contract_product(gradient_row_block, down_weight, 1, 1)
    hidden_gradient = hidden_gradient + adapter_scale_factor * jnp.dot(
        low_rank_gradient, owned_input, preferred_element_type=jnp.float32
    )
    up_grad = (hidden_gradient * gate_pre * sigmoid_gate).astype(jnp.bfloat16)
    gate_grad = (
        hidden_gradient * up_pre * sigmoid_gate * (1.0 + gate_pre * (1.0 - sigmoid_gate))
    ).astype(jnp.bfloat16)
    back_rows = (
        contract_product(gate_grad, gate_weight, 1, 1) + contract_product(up_grad, up_weight, 1, 1)
    ).astype(jnp.bfloat16)
    incoming_gradient = adapter_scale_factor * contract_product(
        low_rank_gradient, hidden_state, 0, 0
    )
    outgoing_gradient = adapter_scale_factor * contract_product(
        low_rank_input, gradient_row_block, 0, 0
    )
    back_block = back_rows.reshape(dp_count, expert_count, capacity, width)
    returned = lax.all_to_all(
        lax.all_to_all(back_block, "dp", split_axis=0, concat_axis=0, tiled=True),
        "expert",
        split_axis=1,
        concat_axis=1,
        tiled=True,
    )
    per_row = jnp.take(returned.reshape(buffer_size, width), position, axis=0)
    input_grad = jnp.sum(
        per_row.reshape(token_count, top_count, width).astype(jnp.float32), axis=1
    ).astype(jnp.bfloat16)
    selector = (jnp.arange(local_experts, dtype=jnp.int32) == hosted_local).astype(jnp.float32)
    placed_in = selector[:, None, None] * incoming_gradient[None, :, :]
    placed_out = selector[:, None, None] * outgoing_gradient[None, :, :]
    summed_in, summed_out = (
        lax.psum_scatter(placed_in, "dp", scatter_dimension=1, tiled=True),
        lax.psum_scatter(placed_out, "dp", scatter_dimension=1, tiled=True),
    )
    step_in, momentum_in, variance_in = adamw(adapter_in, summed_in, moment_in, second_in)
    step_out, momentum_out, variance_out = adamw(adapter_out, summed_out, moment_out, second_out)
    copied_in, copied_out = (
        lax.all_gather(step_in.astype(jnp.bfloat16), "dp", axis=1, tiled=True),
        lax.all_gather(step_out.astype(jnp.bfloat16), "dp", axis=1, tiled=True),
    )
    replica_in = lax.dynamic_index_in_dim(copied_in, hosted_local, 0, keepdims=True)
    replica_out = lax.dynamic_index_in_dim(copied_out, hosted_local, 0, keepdims=True)
    return (
        input_grad,
        step_in,
        step_out,
        momentum_in,
        momentum_out,
        variance_in,
        variance_out,
        replica_in,
        replica_out,
    )


def solution(mesh):
    return jax.shard_map(
        per_device,
        mesh=mesh,
        in_specs=(
            P(("dp", "expert"), None),
            P(("dp", "expert"), None),
            P(("dp", "expert"), None),
            P(("dp", "expert"), None),
            P(),
            P(("dp", "expert"), None, None),
            P(("dp", "expert"), None, None),
            P(("dp", "expert"), None, None),
            P("expert", "dp", None),
            P("expert", "dp", None),
            P("expert", "dp", None),
            P("expert", "dp", None),
            P("expert", "dp", None),
            P("expert", "dp", None),
        ),
        out_specs=(
            P(("dp", "expert"), None),
            P("expert", "dp", None),
            P("expert", "dp", None),
            P("expert", "dp", None),
            P("expert", "dp", None),
            P("expert", "dp", None),
            P("expert", "dp", None),
            P(("dp", "expert"), None, None),
            P(("dp", "expert"), None, None),
        ),
        check_vma=False,
    )
```

profile of v0, /device:TPU:1, one launch (start us, length us, event | category | flops | bytes accessed | tf_op | source)
XLA Modules:
  0.0 540.5 jit_solution(13556978153045774076)
XLA Ops:
  16.6 4.3 gather_fusion.2
  20.8 9.1 %gather.26 = bf16[4,64,3,2048]{3,2,1,0:T(4,128)(2,1)} reshape(bf16[768,2048]{1,0:T(8,128)(2,1)} %gather_fusion.2) | data formatting | bytes 6291456 | tf_op jit(solution)/shard_map/jit(_take)/gather | solution.py:39
  30.2 4.1 broadcast_select_fusion
  34.3 4.0 copy.61
  38.3 5.2 all-to-all-start.2
  46.0 8.5 %gather_fusion.1 = bf16[768,2048]{1,0:T(8,128)(2,1)} fusion(bf16[256,2048]{1,0:T(8,128)(2,1)} %fusion.9, s32[1024]{0:T(1024)S(1)} %pad_clamp_fusion.2), kind=kCustom, calls=%fused_computation.1 | custom fusion | bytes 6294528 | tf_op jit(solution)/shard_map/jit(_take)/gather | solution.py:40
  54.6 9.1 %gather.24 = bf16[4,64,3,2048]{3,2,1,0:T(4,128)(2,1)} reshape(bf16[768,2048]{1,0:T(8,128)(2,1)} %gather_fusion.1) | data formatting | bytes 6291456 | tf_op jit(solution)/shard_map/jit(_take)/gather | solution.py:40
  63.6 4.1 broadcast_select_fusion.1
  67.8 4.1 copy.58
  71.8 7.2 %all-to-all-done.2 = bf16[4,64,3,2048]{3,1,2,0:T(8,128)(2,1)} async-done(((bf16[4,64,3,2048]{3,1,2,0:T(8,128)(2,1)}), bf16[4,64,3,2048]{3,1,2,0:T(8,128)(2,1)}, u32[]{:S(2)}, u32[]{:S(2)}) %all-to-all-start.2) | async-done | bytes 3145760 | tf_op jit(solution)/shard_map/all_to_all | solution.py:96
  79.0 4.7 all-to-all-start
  83.6 6.1 %copy.62 = bf16[4,64,3,2048]{3,0,2,1:T(4,128)(2,1)} copy(bf16[4,64,3,2048]{3,1,2,0:T(8,128)(2,1)} %all-to-all-done.2) | data formatting | bytes 6291456 | tf_op jit(solution)/shard_map/all_to_all | solution.py:96
  89.7 28.1 %all-to-all-done = bf16[4,64,3,2048]{3,1,2,0:T(8,128)(2,1)} async-done(((bf16[4,64,3,2048]{3,1,2,0:T(8,128)(2,1)}), bf16[4,64,3,2048]{3,1,2,0:T(8,128)(2,1)}, u32[]{:S(2)}, u32[]{:S(2)}) %all-to-all-start) | async-done | bytes 3145760 | tf_op jit(solution)/shard_map/all_to_all | solution.py:103
  117.8 19.1 %all-to-all-start.3 = ((bf16[4,64,3,2048]{3,0,2,1:T(4,128)(2,1)}), bf16[4,64,3,2048]{3,0,2,1:T(4,128)(2,1)}, u32[]{:S(2)}, u32[]{:S(2)}) async-start(bf16[4,64,3,2048]{3,0,2,1:T(4,128)(2,1)} %copy.62), calls=%async_computation.3 | async-start | bytes 6291456 | tf_op jit(solution)/shard_map/all_to_all | solution.py:95
  136.8 6.0 %copy.59 = bf16[4,64,3,2048]{3,0,2,1:T(4,128)(2,1)} copy(bf16[4,64,3,2048]{3,1,2,0:T(8,128)(2,1)} %all-to-all-done) | data formatting | bytes 6291456 | tf_op jit(solution)/shard_map/all_to_all | solution.py:103
  142.8 67.2 %all-to-all-done.3 = bf16[4,64,3,2048]{3,0,2,1:T(4,128)(2,1)} async-done(((bf16[4,64,3,2048]{3,0,2,1:T(4,128)(2,1)}), bf16[4,64,3,2048]{3,0,2,1:T(4,128)(2,1)}, u32[]{:S(2)}, u32[]{:S(2)}) %all-to-all-start.3) | async-done | bytes 3145760 | tf_op jit(solution)/shard_map/all_to_all | solution.py:95
  210.1 6.3 %all-to-all-start.1 = ((bf16[4,64,3,2048]{3,0,2,1:T(4,128)(2,1)}), bf16[4,64,3,2048]{3,0,2,1:T(4,128)(2,1)}, u32[]{:S(2)}, u32[]{:S(2)}) async-start(bf16[4,64,3,2048]{3,0,2,1:T(4,128)(2,1)} %copy.59), calls=%async_computation.1 | async-start | bytes 6291456 | tf_op jit(solution)/shard_map/all_to_all | solution.py:102
  218.4 10.4 %all_gather.13 = bf16[2,64,768]{2,1,0:T(8,128)(2,1)S(1)} all-gather(bf16[2,16,768]{2,1,0:T(8,128)(2,1)S(1)} %convert_element_type.60), channel_id=1, replica_groups=mesh['dp'=4,'expert'=64] {'dp'}, dimensions={1}, use_global_device_ids=true | all-gather | bytes 245760 | tf_op jit(solution)/shard_map/all_gather | solution.py:111
  228.8 6.5 %copy.63 = bf16[4,64,3,2048]{3,2,1,0:T(4,128)(2,1)} copy(bf16[4,64,3,2048]{3,0,2,1:T(4,128)(2,1)} %all-to-all-done.3) | data formatting | bytes 6291456 | tf_op jit(solution)/shard_map/all_to_all | solution.py:95
  235.4 9.0 %reshape.237 = bf16[768,2048]{1,0:T(8,128)(2,1)} reshape(bf16[4,64,3,2048]{3,2,1,0:T(4,128)(2,1)} %copy.63) | data formatting | bytes 6291456 | tf_op jit(solution)/shard_map/reshape | solution.py:117
  244.3 45.5 %all-to-all-done.1 = bf16[4,64,3,2048]{3,0,2,1:T(4,128)(2,1)} async-done(((bf16[4,64,3,2048]{3,0,2,1:T(4,128)(2,1)}), bf16[4,64,3,2048]{3,0,2,1:T(4,128)(2,1)}, u32[]{:S(2)}, u32[]{:S(2)}) %all-to-all-start.1) | async-done | bytes 3145760 | tf_op jit(solution)/shard_map/all_to_all | solution.py:102
  289.8 6.5 %copy.60 = bf16[4,64,3,2048]{3,2,1,0:T(4,128)(2,1)} copy(bf16[4,64,3,2048]{3,0,2,1:T(4,128)(2,1)} %all-to-all-done.1) | data formatting | bytes 6291456 | tf_op jit(solution)/shard_map/all_to_all | solution.py:102
  296.3 8.8 %reshape.236 = bf16[768,2048]{1,0:T(8,128)(2,1)} reshape(bf16[4,64,3,2048]{3,2,1,0:T(4,128)(2,1)} %copy.60) | data formatting | bytes 6291456 | tf_op jit(solution)/shard_map/reshape | solution.py:118
  305.2 5.6 %fusion.2 = f32[768,768]{1,0:T(8,128)S(1)} fusion(bf16[768,2048]{1,0:T(8,128)(2,1)} %reshape.237, bf16[1,2048,768]{2,1,0:T(8,128)(2,1)} %param.19), kind=kOutput, calls=%fused_computation.10 | convolution fusion | flops 2415919104 | bytes 8650752 | tf_op jit(solution)/shard_map/dot_general | solution.py:122
  310.8 4.5 multiply_convert_fusion
  315.3 4.2 convolution_multiply_fusion
  319.5 2.2 broadcast_multiply_fusion
  321.8 6.9 %fusion.7 = f32[768,768]{1,0:T(8,128)} fusion(bf16[768,2048]{1,0:T(8,128)(2,1)} %reshape.236, bf16[1,768,2048]{2,1,0:T(8,128)(2,1)} %param.21), kind=kOutput, calls=%fused_computation.15 | convolution fusion | flops 2415919104 | bytes 8650752 | tf_op jit(solution)/shard_map/dot_general | solution.py:15
  328.7 12.9 %reduce-scatter.5.cloned.1.call-done = f32[2,16,2048]{2,1,0:T(8,128)} async-done(((f32[2,64,2048]{2,1,0:T(8,128)}), f32[2,16,2048]{2,1,0:T(8,128)}) %reduce-scatter.5.cloned.1.call-update) | async-done | bytes 262160 | tf_op jit(solution)/shard_map/reduce_scatter | solution.py:162
  341.6 2.3 fusion.39
  343.9 11.2 %all_gather.12 = bf16[2,64,2048]{2,1,0:T(8,128)(2,1)S(1)} all-gather(bf16[2,16,2048]{2,1,0:T(8,128)(2,1)S(1)} %get-tuple-element.23), channel_id=1, replica_groups=mesh['dp'=4,'expert'=64] {'dp'}, dimensions={1}, use_global_device_ids=true | all-gather | bytes 655360 | tf_op jit(solution)/shard_map/all_gather | solution.py:112
  355.1 3.1 convolution_convert_fusion.1
  360.1 3.3 fusion
  363.5 4.1 add_convert_fusion
  367.5 9.1 %reshape.238 = bf16[4,64,3,2048]{3,2,1,0:T(4,128)(2,1)} reshape(bf16[768,2048]{1,0:T(8,128)(2,1)} %add_convert_fusion) | data formatting | bytes 6291456 | tf_op jit(solution)/shard_map/reshape | solution.py:145
  376.6 4.5 copy.64
  381.1 36.2 %all_to_all.30 = bf16[4,64,3,2048]{3,1,2,0:T(8,128)(2,1)S(1)} all-to-all(bf16[4,64,3,2048]{3,1,2,0:T(8,128)(2,1)S(1)} %copy.64), channel_id=1, replica_groups=mesh['dp'=4,'expert'=64] {'dp'}, dimensions={0} | all-to-all | bytes 6291456 | tf_op jit(solution)/shard_map/all_to_all | solution.py:147
  417.3 4.1 copy.65
  421.4 15.0 %all-to-all-start.5 = ((bf16[4,64,3,2048]{3,0,2,1:T(4,128)(2,1)}), bf16[4,64,3,2048]{3,0,2,1:T(4,128)(2,1)}, u32[]{:S(2)}, u32[]{:S(2)}) async-start(bf16[4,64,3,2048]{3,0,2,1:T(4,128)(2,1)} %copy.65), calls=%async_computation.5 | async-start | bytes 6291456 | tf_op jit(solution)/shard_map/all_to_all | solution.py:146
  439.2 11.1 %all_gather.15 = bf16[2,64,2048]{2,1,0:T(8,128)(2,1)S(1)} all-gather(bf16[2,16,2048]{2,1,0:T(8,128)(2,1)S(1)} %copy-done.4), channel_id=1, replica_groups=mesh['dp'=4,'expert'=64] {'dp'}, dimensions={1}, use_global_device_ids=true | all-gather | bytes 655360 | tf_op jit(solution)/shard_map/all_gather | solution.py:168
  451.0 10.1 %reduce-scatter.3.cloned.1.call-done = f32[2,16,768]{2,1,0:T(8,128)} async-done(((f32[2,64,768]{2,1,0:T(8,128)}), f32[2,16,768]{2,1,0:T(8,128)}) %reduce-scatter.3.cloned.1.call-update) | async-done | bytes 98320 | tf_op jit(solution)/shard_map/reduce_scatter | solution.py:161
  461.0 1.7 fusion.41
  462.8 10.7 %all_gather.14 = bf16[2,64,768]{2,1,0:T(8,128)(2,1)S(1)} all-gather(bf16[2,16,768]{2,1,0:T(8,128)(2,1)S(1)} %get-tuple-element.13), channel_id=1, replica_groups=mesh['dp'=4,'expert'=64] {'dp'}, dimensions={1}, use_global_device_ids=true | all-gather | bytes 245760 | tf_op jit(solution)/shard_map/all_gather | solution.py:167
  474.1 35.7 %all-to-all-done.5 = bf16[4,64,3,2048]{3,0,2,1:T(4,128)(2,1)} async-done(((bf16[4,64,3,2048]{3,0,2,1:T(4,128)(2,1)}), bf16[4,64,3,2048]{3,0,2,1:T(4,128)(2,1)}, u32[]{:S(2)}, u32[]{:S(2)}) %all-to-all-start.5) | async-done | bytes 3145760 | tf_op jit(solution)/shard_map/all_to_all | solution.py:146
  509.8 6.5 %copy.66 = bf16[4,64,3,2048]{3,2,1,0:T(4,128)(2,1)} copy(bf16[4,64,3,2048]{3,0,2,1:T(4,128)(2,1)} %all-to-all-done.5) | data formatting | bytes 6291456 | tf_op jit(solution)/shard_map/all_to_all | solution.py:146
  516.3 8.8 %reshape.239 = bf16[768,2048]{1,0:T(8,128)(2,1)} reshape(bf16[4,64,3,2048]{3,2,1,0:T(4,128)(2,1)} %copy.66) | data formatting | bytes 6291456 | tf_op jit(solution)/shard_map/reshape | solution.py:153
  525.1 5.6 %gather_fusion.3 = bf16[256,2048]{1,0:T(8,128)(2,1)} fusion(bf16[768,2048]{1,0:T(8,128)(2,1)} %reshape.239, s32[1024]{0:T(1024)S(1)} %pad_clamp_fusion), kind=kCustom, calls=%fused_computation.3 | custom fusion | bytes 2098176 | tf_op jit(solution)/shard_map/jit(_take)/gather | solution.py:153
  530.8 2.4 fusion.12
  (82 shorter events, 19.4 us)
Async XLA Ops:
  7.2 303.6 %copy-start = (bf16[1,2048,768]{2,1,0:T(8,128)(2,1)S(1)}, bf16[1,2048,768]{2,1,0:T(8,128)(2,1)}, u32[]{:S(2)}) copy-start(bf16[1,2048,768]{2,1,0:T(8,128)(2,1)} %param.20) | copy-start | bytes 9437188
  7.2 9.4 %copy-start.1 = (bf16[32,2048]{1,0:T(8,128)(2,1)S(1)}, bf16[32,2048]{1,0:T(8,128)(2,1)}, u32[]{:S(2)}) copy-start(bf16[32,2048]{1,0:T(8,128)(2,1)} %param.14) | copy-start | bytes 393220
  11.4 0.6 copy-start.6
  13.9 7.0 %copy-start.8 = (s32[256]{0:T(256)}, s32[256]{0:T(256)S(1)}, u32[]{:S(2)}) copy-start(s32[256]{0:T(256)S(1)} %broadcast_multiply_fusion.2) | copy-start | bytes 3076
  14.6 0.6 copy-start.11
  38.3 6.4 %copy-start.10 = (f32[32,8]{0,1:T(8,128)S(1)}, f32[32,8]{0,1:T(8,128)}, u32[]{:S(2)}) copy-start(f32[32,8]{0,1:T(8,128)} %param.16) | copy-start | bytes 3076
  38.3 40.7 %all-to-all-start.2 = ((bf16[4,64,3,2048]{3,1,2,0:T(8,128)(2,1)}), bf16[4,64,3,2048]{3,1,2,0:T(8,128)(2,1)}, u32[]{:S(2)}, u32[]{:S(2)}) async-start(bf16[4,64,3,2048]{3,1,2,0:T(8,128)(2,1)} %copy.61), calls=%async_computation.2 | async-start | bytes 6291456 | tf_op jit(solution)/shard_map/all_to_all | solution.py:96
  79.0 38.8 %all-to-all-start = ((bf16[4,64,3,2048]{3,1,2,0:T(8,128)(2,1)}), bf16[4,64,3,2048]{3,1,2,0:T(8,128)(2,1)}, u32[]{:S(2)}, u32[]{:S(2)}) async-start(bf16[4,64,3,2048]{3,1,2,0:T(8,128)(2,1)} %copy.58), calls=%async_computation | async-start | bytes 6291456 | tf_op jit(solution)/shard_map/all_to_all | solution.py:103
  117.8 92.3 %all-to-all-start.3 = ((bf16[4,64,3,2048]{3,0,2,1:T(4,128)(2,1)}), bf16[4,64,3,2048]{3,0,2,1:T(4,128)(2,1)}, u32[]{:S(2)}, u32[]{:S(2)}) async-start(bf16[4,64,3,2048]{3,0,2,1:T(4,128)(2,1)} %copy.62), calls=%async_computation.3 | async-start | bytes 6291456 | tf_op jit(solution)/shard_map/all_to_all | solution.py:95
  142.8 75.5 %copy-start.5 = (f32[2,16,768]{2,1,0:T(8,128)S(1)}, f32[2,16,768]{2,1,0:T(8,128)}, u32[]{:S(2)}) copy-start(f32[2,16,768]{2,1,0:T(8,128)} %param.22) | copy-start | bytes 294916
  210.1 79.7 %all-to-all-start.1 = ((bf16[4,64,3,2048]{3,0,2,1:T(4,128)(2,1)}), bf16[4,64,3,2048]{3,0,2,1:T(4,128)(2,1)}, u32[]{:S(2)}, u32[]{:S(2)}) async-start(bf16[4,64,3,2048]{3,0,2,1:T(4,128)(2,1)} %copy.59), calls=%async_computation.1 | async-start | bytes 6291456 | tf_op jit(solution)/shard_map/all_to_all | solution.py:102
  216.4 125.2 %reduce-scatter.5.cloned.1.call-start = ((), (), s32[]{:S(2)}) async-start(), calls=%async_computation.9 | async-start | bytes 1310720 | tf_op jit(solution)/shard_map/reduce_scatter | solution.py:162
  228.8 90.7 %copy-start.13 = (f32[2]{0:T(128)}, f32[2]{0:T(128)S(1)}, u32[]{:S(2)}) copy-start(f32[2]{0:T(128)S(1)} %compare_convert_fusion) | copy-start | bytes 28
  305.2 5.6 %copy-start.2 = (bf16[768,2048]{1,0:T(8,128)(2,1)S(1)}, bf16[768,2048]{1,0:T(8,128)(2,1)}, u32[]{:S(2)}) copy-start(bf16[768,2048]{1,0:T(8,128)(2,1)} %reshape.237) | copy-start | bytes 9437188
  310.8 4.5 copy-start.16
  343.9 14.3 %copy-start.3 = (f32[768,768]{1,0:T(8,128)S(1)}, f32[768,768]{1,0:T(8,128)}, u32[]{:S(2)}) copy-start(f32[768,768]{1,0:T(8,128)} %fusion.7) | copy-start | bytes 7077892
  355.1 3.6 copy-start.17
  355.1 3.6 copy-start.18
  358.2 1.9 copy-start.15
  421.4 16.6 %copy-start.14 = (f32[2]{0:T(128)S(1)}, f32[2]{0:T(128)}, u32[]{:S(2)}) copy-start(f32[2]{0:T(128)} %copy-done.13) | copy-start | bytes 28
  421.4 17.5 %copy-start.9 = (s32[256]{0:T(256)S(1)}, s32[256]{0:T(256)}, u32[]{:S(2)}) copy-start(s32[256]{0:T(256)} %copy-done.8) | copy-start | bytes 3076
  421.4 17.6 %copy-start.7 = (s32[256]{0:T(256)S(1)}, s32[256]{0:T(256)}, u32[]{:S(2)}) copy-start(s32[256]{0:T(256)} %convert_reduce_fusion) | copy-start | bytes 3076
  421.4 17.7 %copy-start.12 = (s32[256,1]{0,1:T(1,128)S(1)}, s32[256,1]{0,1:T(1,128)}, u32[]{:S(2)}) copy-start(s32[256,1]{0,1:T(1,128)} %copy-done.11) | copy-start | bytes 3076
  421.4 17.8 %copy-start.4 = (bf16[2,16,2048]{2,1,0:T(8,128)(2,1)S(1)}, bf16[2,16,2048]{2,1,0:T(8,128)(2,1)}, u32[]{:S(2)}) copy-start(bf16[2,16,2048]{2,1,0:T(8,128)(2,1)} %get-tuple-element.9) | copy-start | bytes 393220
  421.4 88.4 %all-to-all-start.5 = ((bf16[4,64,3,2048]{3,0,2,1:T(4,128)(2,1)}), bf16[4,64,3,2048]{3,0,2,1:T(4,128)(2,1)}, u32[]{:S(2)}, u32[]{:S(2)}) async-start(bf16[4,64,3,2048]{3,0,2,1:T(4,128)(2,1)} %copy.65), calls=%async_computation.5 | async-start | bytes 6291456 | tf_op jit(solution)/shard_map/all_to_all | solution.py:146
  436.3 24.7 %reduce-scatter.3.cloned.1.call-start = ((), (), s32[]{:S(2)}) async-start(), calls=%async_computation.8 | async-start | bytes 491520 | tf_op jit(solution)/shard_map/reduce_scatter | solution.py:161
Sparse Core Ops, SparseCore 0:
  321.9 19.6 reduce-scatter.4
  439.9 21.1 reduce-scatter.2
where the time goes:
time: 549 us; the launch traced here: 540 us
  waiting for transfers between devices  207 us (38%)
  local copies, waits for them, and re-layouts  131 us (24%)
  blocking collectives  79.6 us (14%)
  starting transfers between devices  50.2 us (9%)
  matrix products  33.8 us (6%)
  other arithmetic  24 us (4%)
  between operations  15.5 us (3%)
    all_to_all x1, waiting for transfers between devices, per_device(): lax.all_to_all(lax.all_to_all(send_input, 'dp', split_axis=0, concat_axis...  67.2 us
    all_to_all x1, waiting for transfers between devices, per_device(): lax.all_to_all(lax.all_to_all(send_grad, 'dp', split_axis=0, concat_axis=...  45.5 us
    all_to_all x1, blocking collectives, per_device(): lax.all_to_all(back_block, 'dp', split_axis=0, concat_axis=0, tiled=True)  36.2 us
    all_to_all x1, waiting for transfers between devices, per_device(): lax.all_to_all(lax.all_to_all(back_block, 'dp', split_axis=0, concat_axis...  35.7 us
    all_to_all x1, waiting for transfers between devices, per_device(): lax.all_to_all(send_grad, 'dp', split_axis=0, concat_axis=0, tiled=True)  28.1 us
    dot_general x6, matrix products, contract_product(): lax.dot_general(left, right, (((left_dim,), (right_dim,)), ((), ())), pre...  23.2 us
    all_to_all x1, starting transfers between devices, per_device(): lax.all_to_all(lax.all_to_all(send_input, 'dp', split_axis=0, concat_axis...  19.1 us
    gather x2, local copies, waits for them, and re-layouts, pack_rows(): send_grad = jnp.take(scaled, filler, axis=0, mode='fill', fill_value=0)  17.6 us
  transfers between devices with their start and end apart: 7, of which 7 were waited for; matrix products, arithmetic and copies ran while one was open for 13% of the time, Pallas kernels for 0%

commit v1 on v0

--- a/solution.py
+++ b/solution.py
@@ -9,6 +9,22 @@
 beta_two = 0.999
 decay_rate = 0.01
 adam_eps = 1e-08
+
+
+def gather_around(x, axis, dim):
+    ways, here, step = (lax.axis_size(axis), lax.axis_index(axis), x.shape[dim])
+    shape = [n * ways if d == dim else n for d, n in enumerate(x.shape)]
+    full = lax.dynamic_update_slice_in_dim(jnp.zeros(shape, x.dtype), x, here * step, axis=dim)
+    going_up = going_down = x
+    for far in range(1, ways // 2 + 1):
+        going_up = lax.ppermute(going_up, axis, [(d, (d + 1) % ways) for d in range(ways)])
+        full = lax.dynamic_update_slice_in_dim(full, going_up, (here - far) % ways * step, axis=dim)
+        if 2 * far < ways:
+            going_down = lax.ppermute(going_down, axis, [(d, (d - 1) % ways) for d in range(ways)])
+            full = lax.dynamic_update_slice_in_dim(
+                full, going_down, (here + far) % ways * step, axis=dim
+            )
+    return full
 
 
 def contract_product(left, right, left_dim, right_dim):
@@ -165,7 +181,7 @@
     step_out, momentum_out, variance_out = adamw(adapter_out, summed_out, moment_out, second_out)
     copied_in, copied_out = (
         lax.all_gather(step_in.astype(jnp.bfloat16), "dp", axis=1, tiled=True),
-        lax.all_gather(step_out.astype(jnp.bfloat16), "dp", axis=1, tiled=True),
+        gather_around(step_out.astype(jnp.bfloat16), "dp", 1),
     )
     replica_in = lax.dynamic_index_in_dim(copied_in, hosted_local, 0, keepdims=True)
     replica_out = lax.dynamic_index_in_dim(copied_out, hosted_local, 0, keepdims=True)

time: 549 us -> 539 us (0.982)
  blocking collectives: 79.6 us -> 67.9 us
    all_to_all x1, waiting for transfers between devices: 35.7 us -> 20.5 us  [per_device(): lax.all_to_all(lax.all_to_all(back_block, 'dp', split_axis=0, concat_axis...]
    all_gather x1 -> x0, blocking collectives: 11.1 us -> none  [per_device(): lax.all_gather(step_out.astype(jnp.bfloat16), 'dp', axis=1, tiled=True)]
    reduce_scatter x1, waiting for transfers between devices: 12.9 us -> 23.7 us  [per_device(): lax.psum_scatter(placed_out, 'dp', scatter_dimension=1, tiled=True)]
  transfers between devices with their start and end apart: 7 -> 10, of which waited for: 7 -> 9; matrix products, arithmetic and copies ran while one was open for 13% -> 14% of each run, Pallas kernels for 0% -> 0%
where the time goes in v1:
time: 539 us; the launch traced here: 530 us
  waiting for transfers between devices  205 us (38%)
  local copies, waits for them, and re-layouts  129 us (24%)
  blocking collectives  67.9 us (13%)
  starting transfers between devices  53.8 us (10%)
  matrix products  33.7 us (6%)
  other arithmetic  24.7 us (5%)
  between operations  15.6 us (3%)
    all_to_all x1, waiting for transfers between devices, per_device(): lax.all_to_all(lax.all_to_all(send_input, 'dp', split_axis=0, concat_axis...  67.2 us
    all_to_all x1, waiting for transfers between devices, per_device(): lax.all_to_all(lax.all_to_all(send_grad, 'dp', split_axis=0, concat_axis=...  43.6 us
    all_to_all x1, blocking collectives, per_device(): lax.all_to_all(back_block, 'dp', split_axis=0, concat_axis=0, tiled=True)  35 us
    all_to_all x1, waiting for transfers between devices, per_device(): lax.all_to_all(send_grad, 'dp', split_axis=0, concat_axis=0, tiled=True)  28.2 us
    reduce_scatter x1, waiting for transfers between devices, per_device(): lax.psum_scatter(placed_out, 'dp', scatter_dimension=1, tiled=True)  23.7 us
    dot_general x6, matrix products, contract_product(): lax.dot_general(left, right, (((left_dim,), (right_dim,)), ((), ())), pre...  21.7 us
    all_to_all x1, waiting for transfers between devices, per_device(): lax.all_to_all(lax.all_to_all(back_block, 'dp', split_axis=0, concat_axis...  20.5 us
    all_to_all x1, starting transfers between devices, per_device(): lax.all_to_all(lax.all_to_all(send_input, 'dp', split_axis=0, concat_axis...  19.1 us
  transfers between devices with their start and end apart: 10, of which 9 were waited for; matrix products, arithmetic and copies ran while one was open for 14% of the time, Pallas kernels for 0%

profile of v1, /device:TPU:1, one launch (start us, length us, event | category | flops | bytes accessed | tf_op | source)
XLA Modules:
  0.0 530.1 jit_solution(3820169630055768124)
XLA Ops:
  16.6 4.2 gather_fusion.2
  20.8 9.1 %gather.26 = bf16[4,64,3,2048]{3,2,1,0:T(4,128)(2,1)} reshape(bf16[768,2048]{1,0:T(8,128)(2,1)} %gather_fusion.2) | data formatting | bytes 6291456 | tf_op jit(solution)/shard_map/jit(_take)/gather | solution.py:55
  30.2 4.1 broadcast_select_fusion
  34.3 4.0 copy.61
  38.3 5.2 all-to-all-start.2
  46.0 8.5 %gather_fusion.1 = bf16[768,2048]{1,0:T(8,128)(2,1)} fusion(bf16[256,2048]{1,0:T(8,128)(2,1)} %fusion.9, s32[1024]{0:T(1024)S(1)} %pad_clamp_fusion.2), kind=kCustom, calls=%fused_computation.1 | custom fusion | bytes 6294528 | tf_op jit(solution)/shard_map/jit(_take)/gather | solution.py:56
  54.5 9.1 %gather.24 = bf16[4,64,3,2048]{3,2,1,0:T(4,128)(2,1)} reshape(bf16[768,2048]{1,0:T(8,128)(2,1)} %gather_fusion.1) | data formatting | bytes 6291456 | tf_op jit(solution)/shard_map/jit(_take)/gather | solution.py:56
  63.6 4.1 broadcast_select_fusion.1
  67.7 4.0 copy.58
  71.8 7.2 %all-to-all-done.2 = bf16[4,64,3,2048]{3,1,2,0:T(8,128)(2,1)} async-done(((bf16[4,64,3,2048]{3,1,2,0:T(8,128)(2,1)}), bf16[4,64,3,2048]{3,1,2,0:T(8,128)(2,1)}, u32[]{:S(2)}, u32[]{:S(2)}) %all-to-all-start.2) | async-done | bytes 3145760 | tf_op jit(solution)/shard_map/all_to_all | solution.py:112
  78.9 4.7 all-to-all-start
  83.6 6.0 %copy.62 = bf16[4,64,3,2048]{3,0,2,1:T(4,128)(2,1)} copy(bf16[4,64,3,2048]{3,1,2,0:T(8,128)(2,1)} %all-to-all-done.2) | data formatting | bytes 6291456 | tf_op jit(solution)/shard_map/all_to_all | solution.py:112
  89.6 28.2 %all-to-all-done = bf16[4,64,3,2048]{3,1,2,0:T(8,128)(2,1)} async-done(((bf16[4,64,3,2048]{3,1,2,0:T(8,128)(2,1)}), bf16[4,64,3,2048]{3,1,2,0:T(8,128)(2,1)}, u32[]{:S(2)}, u32[]{:S(2)}) %all-to-all-start) | async-done | bytes 3145760 | tf_op jit(solution)/shard_map/all_to_all | solution.py:119
  117.8 19.1 %all-to-all-start.3 = ((bf16[4,64,3,2048]{3,0,2,1:T(4,128)(2,1)}), bf16[4,64,3,2048]{3,0,2,1:T(4,128)(2,1)}, u32[]{:S(2)}, u32[]{:S(2)}) async-start(bf16[4,64,3,2048]{3,0,2,1:T(4,128)(2,1)} %copy.62), calls=%async_computation.3 | async-start | bytes 6291456 | tf_op jit(solution)/shard_map/all_to_all | solution.py:111
  136.8 6.0 %copy.59 = bf16[4,64,3,2048]{3,0,2,1:T(4,128)(2,1)} copy(bf16[4,64,3,2048]{3,1,2,0:T(8,128)(2,1)} %all-to-all-done) | data formatting | bytes 6291456 | tf_op jit(solution)/shard_map/all_to_all | solution.py:119
  142.8 67.2 %all-to-all-done.3 = bf16[4,64,3,2048]{3,0,2,1:T(4,128)(2,1)} async-done(((bf16[4,64,3,2048]{3,0,2,1:T(4,128)(2,1)}), bf16[4,64,3,2048]{3,0,2,1:T(4,128)(2,1)}, u32[]{:S(2)}, u32[]{:S(2)}) %all-to-all-start.3) | async-done | bytes 3145760 | tf_op jit(solution)/shard_map/all_to_all | solution.py:111
  210.1 6.3 %all-to-all-start.1 = ((bf16[4,64,3,2048]{3,0,2,1:T(4,128)(2,1)}), bf16[4,64,3,2048]{3,0,2,1:T(4,128)(2,1)}, u32[]{:S(2)}, u32[]{:S(2)}) async-start(bf16[4,64,3,2048]{3,0,2,1:T(4,128)(2,1)} %copy.59), calls=%async_computation.1 | async-start | bytes 6291456 | tf_op jit(solution)/shard_map/all_to_all | solution.py:118
  219.0 11.7 %all_gather.9 = bf16[2,64,2048]{2,1,0:T(8,128)(2,1)} all-gather(bf16[2,16,2048]{2,1,0:T(8,128)(2,1)} %convert_element_type.58), channel_id=1, replica_groups=mesh['dp'=4,'expert'=64] {'dp'}, dimensions={1}, use_global_device_ids=true | all-gather | bytes 655360 | tf_op jit(solution)/shard_map/all_gather | solution.py:128
  230.7 6.5 %copy.63 = bf16[4,64,3,2048]{3,2,1,0:T(4,128)(2,1)} copy(bf16[4,64,3,2048]{3,0,2,1:T(4,128)(2,1)} %all-to-all-done.3) | data formatting | bytes 6291456 | tf_op jit(solution)/shard_map/all_to_all | solution.py:111
  237.3 9.0 %reshape.237 = bf16[768,2048]{1,0:T(8,128)(2,1)} reshape(bf16[4,64,3,2048]{3,2,1,0:T(4,128)(2,1)} %copy.63) | data formatting | bytes 6291456 | tf_op jit(solution)/shard_map/reshape | solution.py:133
  246.3 43.6 %all-to-all-done.1 = bf16[4,64,3,2048]{3,0,2,1:T(4,128)(2,1)} async-done(((bf16[4,64,3,2048]{3,0,2,1:T(4,128)(2,1)}), bf16[4,64,3,2048]{3,0,2,1:T(4,128)(2,1)}, u32[]{:S(2)}, u32[]{:S(2)}) %all-to-all-start.1) | async-done | bytes 3145760 | tf_op jit(solution)/shard_map/all_to_all | solution.py:118
  289.8 6.5 %copy.60 = bf16[4,64,3,2048]{3,2,1,0:T(4,128)(2,1)} copy(bf16[4,64,3,2048]{3,0,2,1:T(4,128)(2,1)} %all-to-all-done.1) | data formatting | bytes 6291456 | tf_op jit(solution)/shard_map/all_to_all | solution.py:118
  296.3 8.8 %reshape.236 = bf16[768,2048]{1,0:T(8,128)(2,1)} reshape(bf16[4,64,3,2048]{3,2,1,0:T(4,128)(2,1)} %copy.60) | data formatting | bytes 6291456 | tf_op jit(solution)/shard_map/reshape | solution.py:134
  305.2 5.6 %fusion.2 = f32[768,768]{1,0:T(8,128)S(1)} fusion(bf16[768,2048]{1,0:T(8,128)(2,1)} %reshape.237, bf16[1,2048,768]{2,1,0:T(8,128)(2,1)} %param.19), kind=kOutput, calls=%fused_computation.10 | convolution fusion | flops 2415919104 | bytes 8650752 | tf_op jit(solution)/shard_map/dot_general | solution.py:138
  310.8 4.2 multiply_convert_fusion
  317.3 6.9 %fusion.7 = f32[768,768]{1,0:T(8,128)} fusion(bf16[768,2048]{1,0:T(8,128)(2,1)} %reshape.236, bf16[1,768,2048]{2,1,0:T(8,128)(2,1)} %param.21), kind=kOutput, calls=%fused_computation.15 | convolution fusion | flops 2415919104 | bytes 8650752 | tf_op jit(solution)/shard_map/dot_general | solution.py:31
  324.2 9.5 %reduce-scatter.3.cloned.1.call-done = f32[2,16,768]{2,1,0:T(8,128)} async-done(((f32[2,64,768]{2,1,0:T(8,128)}), f32[2,16,768]{2,1,0:T(8,128)}) %reduce-scatter.3.cloned.1.call-update) | async-done | bytes 98320 | tf_op jit(solution)/shard_map/reduce_scatter | solution.py:177
  333.7 2.0 fusion.40
  335.7 10.1 %all_gather.10 = bf16[2,64,768]{2,1,0:T(8,128)(2,1)S(1)} all-gather(bf16[2,16,768]{2,1,0:T(8,128)(2,1)S(1)} %get-tuple-element.24), channel_id=1, replica_groups=mesh['dp'=4,'expert'=64] {'dp'}, dimensions={1}, use_global_device_ids=true | all-gather | bytes 245760 | tf_op jit(solution)/shard_map/all_gather | solution.py:127
  345.7 2.2 multiply_add_fusion
  348.0 5.0 fusion
  352.9 4.2 add_convert_fusion
  357.1 9.1 %reshape.238 = bf16[4,64,3,2048]{3,2,1,0:T(4,128)(2,1)} reshape(bf16[768,2048]{1,0:T(8,128)(2,1)} %add_convert_fusion) | data formatting | bytes 6291456 | tf_op jit(solution)/shard_map/reshape | solution.py:161
  366.2 4.5 copy.64
  370.7 35.0 %all_to_all.30 = bf16[4,64,3,2048]{3,1,2,0:T(8,128)(2,1)S(1)} all-to-all(bf16[4,64,3,2048]{3,1,2,0:T(8,128)(2,1)S(1)} %copy.64), channel_id=1, replica_groups=mesh['dp'=4,'expert'=64] {'dp'}, dimensions={0} | all-to-all | bytes 6291456 | tf_op jit(solution)/shard_map/all_to_all | solution.py:163
  405.7 4.1 copy.65
  409.8 16.3 %all-to-all-start.5 = ((bf16[4,64,3,2048]{3,0,2,1:T(4,128)(2,1)}), bf16[4,64,3,2048]{3,0,2,1:T(4,128)(2,1)}, u32[]{:S(2)}, u32[]{:S(2)}) async-start(bf16[4,64,3,2048]{3,0,2,1:T(4,128)(2,1)} %copy.65), calls=%async_computation.5 | async-start | bytes 6291456 | tf_op jit(solution)/shard_map/all_to_all | solution.py:162
  426.1 4.3 convolution_multiply_fusion
  430.4 2.2 broadcast_multiply_fusion
  432.9 23.7 %reduce-scatter.5.cloned.1.call-done = f32[2,16,2048]{2,1,0:T(8,128)} async-done(((f32[2,64,2048]{2,1,0:T(8,128)}), f32[2,16,2048]{2,1,0:T(8,128)}) %reduce-scatter.5.cloned.1.call-update) | async-done | bytes 262160 | tf_op jit(solution)/shard_map/reduce_scatter | solution.py:178
  456.7 2.1 constant_dynamic-update-slice_fusion.3
  459.0 11.1 %all_gather.11 = bf16[2,64,768]{2,1,0:T(8,128)(2,1)S(1)} all-gather(bf16[2,16,768]{2,1,0:T(8,128)(2,1)S(1)} %copy-done.9), channel_id=1, replica_groups=mesh['dp'=4,'expert'=64] {'dp'}, dimensions={1}, use_global_device_ids=true | all-gather | bytes 245760 | tf_op jit(solution)/shard_map/all_gather | solution.py:183
  474.7 3.5 collective-permute-done.2
  478.9 20.5 %all-to-all-done.5 = bf16[4,64,3,2048]{3,0,2,1:T(4,128)(2,1)} async-done(((bf16[4,64,3,2048]{3,0,2,1:T(4,128)(2,1)}), bf16[4,64,3,2048]{3,0,2,1:T(4,128)(2,1)}, u32[]{:S(2)}, u32[]{:S(2)}) %all-to-all-start.5) | async-done | bytes 3145760 | tf_op jit(solution)/shard_map/all_to_all | solution.py:162
  499.5 6.5 %copy.66 = bf16[4,64,3,2048]{3,2,1,0:T(4,128)(2,1)} copy(bf16[4,64,3,2048]{3,0,2,1:T(4,128)(2,1)} %all-to-all-done.5) | data formatting | bytes 6291456 | tf_op jit(solution)/shard_map/all_to_all | solution.py:162
  506.0 8.8 %reshape.239 = bf16[768,2048]{1,0:T(8,128)(2,1)} reshape(bf16[4,64,3,2048]{3,2,1,0:T(4,128)(2,1)} %copy.66) | data formatting | bytes 6291456 | tf_op jit(solution)/shard_map/reshape | solution.py:169
  514.8 5.6 %gather_fusion.3 = bf16[256,2048]{1,0:T(8,128)(2,1)} fusion(bf16[768,2048]{1,0:T(8,128)(2,1)} %reshape.239, s32[1024]{0:T(1024)S(1)} %pad_clamp_fusion), kind=kCustom, calls=%fused_computation.3 | custom fusion | bytes 2098176 | tf_op jit(solution)/shard_map/jit(_take)/gather | solution.py:169
  520.4 2.4 fusion.12
  (87 shorter events, 22.2 us)
Async XLA Ops:
  7.2 303.6 %copy-start = (bf16[1,2048,768]{2,1,0:T(8,128)(2,1)S(1)}, bf16[1,2048,768]{2,1,0:T(8,128)(2,1)}, u32[]{:S(2)}) copy-start(bf16[1,2048,768]{2,1,0:T(8,128)(2,1)} %param.20) | copy-start | bytes 9437188
  7.2 9.4 %copy-start.1 = (bf16[32,2048]{1,0:T(8,128)(2,1)S(1)}, bf16[32,2048]{1,0:T(8,128)(2,1)}, u32[]{:S(2)}) copy-start(bf16[32,2048]{1,0:T(8,128)(2,1)} %param.14) | copy-start | bytes 393220
  11.4 0.6 copy-start.8
  14.6 0.6 copy-start.12
  38.3 6.4 %copy-start.11 = (f32[32,8]{0,1:T(8,128)S(1)}, f32[32,8]{0,1:T(8,128)}, u32[]{:S(2)}) copy-start(f32[32,8]{0,1:T(8,128)} %param.16) | copy-start | bytes 3076
  38.3 40.7 %all-to-all-start.2 = ((bf16[4,64,3,2048]{3,1,2,0:T(8,128)(2,1)}), bf16[4,64,3,2048]{3,1,2,0:T(8,128)(2,1)}, u32[]{:S(2)}, u32[]{:S(2)}) async-start(bf16[4,64,3,2048]{3,1,2,0:T(8,128)(2,1)} %copy.61), calls=%async_computation.2 | async-start | bytes 6291456 | tf_op jit(solution)/shard_map/all_to_all | solution.py:112
  78.9 38.8 %all-to-all-start = ((bf16[4,64,3,2048]{3,1,2,0:T(8,128)(2,1)}), bf16[4,64,3,2048]{3,1,2,0:T(8,128)(2,1)}, u32[]{:S(2)}, u32[]{:S(2)}) async-start(bf16[4,64,3,2048]{3,1,2,0:T(8,128)(2,1)} %copy.58), calls=%async_computation | async-start | bytes 6291456 | tf_op jit(solution)/shard_map/all_to_all | solution.py:119
  117.8 92.3 %all-to-all-start.3 = ((bf16[4,64,3,2048]{3,0,2,1:T(4,128)(2,1)}), bf16[4,64,3,2048]{3,0,2,1:T(4,128)(2,1)}, u32[]{:S(2)}, u32[]{:S(2)}) async-start(bf16[4,64,3,2048]{3,0,2,1:T(4,128)(2,1)} %copy.62), calls=%async_computation.3 | async-start | bytes 6291456 | tf_op jit(solution)/shard_map/all_to_all | solution.py:111
  142.8 75.5 %copy-start.6 = (f32[2,16,2048]{2,1,0:T(8,128)S(1)}, f32[2,16,2048]{2,1,0:T(8,128)}, u32[]{:S(2)}) copy-start(f32[2,16,2048]{2,1,0:T(8,128)} %param.23) | copy-start | bytes 786436
  210.1 79.7 %all-to-all-start.1 = ((bf16[4,64,3,2048]{3,0,2,1:T(4,128)(2,1)}), bf16[4,64,3,2048]{3,0,2,1:T(4,128)(2,1)}, u32[]{:S(2)}, u32[]{:S(2)}) async-start(bf16[4,64,3,2048]{3,0,2,1:T(4,128)(2,1)} %copy.59), calls=%async_computation.1 | async-start | bytes 6291456 | tf_op jit(solution)/shard_map/all_to_all | solution.py:118
  216.4 117.3 %reduce-scatter.3.cloned.1.call-start = ((), (), s32[]{:S(2)}) async-start(), calls=%async_computation.8 | async-start | bytes 491520 | tf_op jit(solution)/shard_map/reduce_scatter | solution.py:177
  305.2 5.6 %copy-start.4 = (bf16[768,2048]{1,0:T(8,128)(2,1)S(1)}, bf16[768,2048]{1,0:T(8,128)(2,1)}, u32[]{:S(2)}) copy-start(bf16[768,2048]{1,0:T(8,128)(2,1)} %reshape.237) | copy-start | bytes 9437188
  310.8 4.2 copy-start.15
  310.8 4.2 copy-start.2
  310.8 4.2 copy-start.5
  315.0 1.4 copy-start.3
  333.7 14.3 %copy-start.14 = (bf16[1,2048,768]{2,1,0:T(8,128)(2,1)S(1)}, bf16[1,2048,768]{2,1,0:T(8,128)(2,1)}, u32[]{:S(2)}) copy-start(bf16[1,2048,768]{2,1,0:T(8,128)(2,1)} %param.19) | copy-start | bytes 9437188
  333.7 14.3 %copy-start.16 = (f32[768,768]{1,0:T(8,128)S(1)}, f32[768,768]{1,0:T(8,128)}, u32[]{:S(2)}) copy-start(f32[768,768]{1,0:T(8,128)} %copy-done.15) | copy-start | bytes 7077892
  345.7 7.2 %copy-start.7 = (bf16[2,64,768]{2,1,0:T(8,128)(2,1)}, bf16[2,64,768]{2,1,0:T(8,128)(2,1)S(1)}, u32[]{:S(2)}) copy-start(bf16[2,64,768]{2,1,0:T(8,128)(2,1)S(1)} %all_gather.10) | copy-start | bytes 589828
  409.8 89.7 %all-to-all-start.5 = ((bf16[4,64,3,2048]{3,0,2,1:T(4,128)(2,1)}), bf16[4,64,3,2048]{3,0,2,1:T(4,128)(2,1)}, u32[]{:S(2)}, u32[]{:S(2)}) async-start(bf16[4,64,3,2048]{3,0,2,1:T(4,128)(2,1)} %copy.65), calls=%async_computation.5 | async-start | bytes 6291456 | tf_op jit(solution)/shard_map/all_to_all | solution.py:162
  426.0 6.8 %copy-start.10 = (s32[256]{0:T(256)S(1)}, s32[256]{0:T(256)}, u32[]{:S(2)}) copy-start(s32[256]{0:T(256)} %convert_reduce_fusion) | copy-start | bytes 3076
  426.0 6.8 %copy-start.13 = (s32[256,1]{0,1:T(1,128)S(1)}, s32[256,1]{0,1:T(1,128)}, u32[]{:S(2)}) copy-start(s32[256,1]{0,1:T(1,128)} %copy-done.12) | copy-start | bytes 3076
  426.0 30.6 %reduce-scatter.5.cloned.1.call-start = ((), (), s32[]{:S(2)}) async-start(), calls=%async_computation.9 | async-start | bytes 1310720 | tf_op jit(solution)/shard_map/reduce_scatter | solution.py:178
  430.4 28.6 %copy-start.9 = (bf16[2,16,768]{2,1,0:T(8,128)(2,1)S(1)}, bf16[2,16,768]{2,1,0:T(8,128)(2,1)}, u32[]{:S(2)}) copy-start(bf16[2,16,768]{2,1,0:T(8,128)(2,1)} %get-tuple-element.14) | copy-start | bytes 147460
  458.8 14.0 %collective-permute-start = (bf16[2,16,2048]{2,1,0:T(8,128)(2,1)S(1)}, bf16[2,16,2048]{2,1,0:T(8,128)(2,1)S(1)}, u32[]{:S(2)}, u32[]{:S(2)}) collective-permute-start(bf16[2,16,2048]{2,1,0:T(8,128)(2,1)S(1)} %get-tuple-element.10), channel_id=1, source_target_pairs={{0,64},{64,128},{128,192},{192,0},{1,65},{65,129},{129,193},{193,1... | collective-permute-start | bytes 393224 | tf_op jit(solution)/shard_map/ppermute | solution.py:20
  470.8 3.9 collective-permute-start.1
  472.8 5.4 %collective-permute-start.2 = (bf16[2,16,2048]{2,1,0:T(8,128)(2,1)S(1)}, bf16[2,16,2048]{2,1,0:T(8,128)(2,1)S(1)}, u32[]{:S(2)}, u32[]{:S(2)}) collective-permute-start(bf16[2,16,2048]{2,1,0:T(8,128)(2,1)S(1)} %collective-permute-done), channel_id=1, source_target_pairs={{0,64},{64,128},{128,192},{192,0},{1,65},{65,129},{129,193},{193,1... | collective-permute-start | bytes 393224 | tf_op jit(solution)/shard_map/ppermute | solution.py:20
Sparse Core Ops, SparseCore 0:
  317.4 16.1 reduce-scatter.2
  432.7 23.8 reduce-scatter.4
